TPU v7x, 256 devices: a whole 4x4x8 slice. The times are simulated.
256 devices in a mesh: blk: 64 (over y, x, z_lo, core), grp: 4 (over z_hi).
Axes of the slice: x: 4, y: 4, z: 8 (z_hi: 4, z_lo: 2; z = z_hi * 2 + z_lo), core: 2. Of those that a mesh axis runs over, the one named last changes fastest.
Arguments:
- source_rows: bfloat16 [262144, 400], P(('blk', 'grp')), may hold values from -0.8984375 to 0.8984375
- source_state: float32 [262144], P(('blk', 'grp')), may hold values from 0.002 to 0.02
- target_rows: bfloat16 [262144, 400], P(('blk', 'grp')), may hold values from -0.8984375 to 0.8984375
- target_state: float32 [262144], P(('blk', 'grp')), may hold values from 0.002 to 0.02
- relations: float32 [1024, 400], replicated, may hold values from -6 to 6
- relation_state: float32 [1024], replicated, may hold values from 0.01 to 0.1
- source_ids: int32 [524288], P(('blk', 'grp')), may hold values from 0 to 1023
- relation_ids: int32 [524288], P(('blk', 'grp')), may hold values from 0 to 1023
- target_ids: int32 [524288], P(('blk', 'grp')), may hold values from 0 to 1023
- source_negs: int32 [4096, 1024], P(('blk', 'grp')), may hold values from 0 to 1023
- target_negs: int32 [4096, 1024], P(('blk', 'grp')), may hold values from 0 to 1023
- edge_counts: int32 [256], P(('blk', 'grp')), may hold values from 256 to 2048, as said below
Outputs:
- source_out: bfloat16 [262144, 400], P(('blk', 'grp'))
- source_state_out: float32 [262144], P(('blk', 'grp'))
- target_out: bfloat16 [262144, 400], P(('blk', 'grp'))
- target_state_out: float32 [262144], P(('blk', 'grp'))
- relations_out: float32 [1024, 400], replicated
- relation_state_out: float32 [1024], replicated
Inputs may be any that keep to these rules, and one draw needn't show every extreme that they name: `edge_counts`: each bucket's count is 2048, 1024, 512 or 256, so whole blocks are live; in every draw some bucket has 2048.
All inputs are finite; a program needn't handle non-finite values.
Results may differ from a plain program's by a relative error of at most 0.0016.
Values may be sent and summed in bfloat16 or wider, within the bound.
A program may use at most 64 MiB of HBM per device.

v0:
```python
import jax
import jax.numpy as jnp
from jax import lax
from jax.sharding import PartitionSpec as P

BLOCK = 128


learn_rate = 0.1


def swapped(block, axis, distance):
    count = lax.axis_size(axis)
    route = []
    for low in range(count):
        high = low | 1 << distance
        if high != low and high < count:
            route += [(low, high), (high, low)]
    return lax.ppermute(block, axis, route)


def split_halves(values):
    middle = values.shape[-1] // 2
    return (values[..., :middle], values[..., middle:])


def complex_product(left, right):
    left_re, left_im = split_halves(left)
    right_re, right_im = split_halves(right)
    return jnp.concatenate(
        [left_re * right_re - left_im * right_im, left_re * right_im + left_im * right_re], axis=-1
    )


def conj_product(left, right):
    left_re, left_im = split_halves(left)
    right_re, right_im = split_halves(right)
    return jnp.concatenate(
        [left_re * right_re + left_im * right_im, left_im * right_re - left_re * right_im], axis=-1
    )


def block_step(block, carry, tables):
    (
        source_rows,
        target_rows,
        relations,
        source_ids,
        relation_ids,
        target_ids,
        source_negs,
        target_negs,
    ) = tables
    source_grad, target_grad, relation_grad = carry
    first = (block * BLOCK).astype(jnp.int32)
    pick_source = lax.dynamic_slice_in_dim(source_ids, first, BLOCK)
    pick_relation = lax.dynamic_slice_in_dim(relation_ids, first, BLOCK)
    pick_target = lax.dynamic_slice_in_dim(target_ids, first, BLOCK)
    source_vec = jnp.take(source_rows, pick_source, axis=0).astype(jnp.float32)
    target_vec = jnp.take(target_rows, pick_target, axis=0).astype(jnp.float32)
    relation_vec = jnp.take(relations, pick_relation, axis=0)
    query = complex_product(source_vec, relation_vec)
    probe = conj_product(relation_vec, target_vec)
    positive = jnp.sum(query * target_vec, axis=-1)
    query_low = query.astype(jnp.bfloat16)
    probe_low = probe.astype(jnp.bfloat16)
    neg_target_ids = target_negs[block]
    neg_source_ids = source_negs[block]
    neg_target = jnp.take(target_rows, neg_target_ids, axis=0)
    neg_source = jnp.take(source_rows, neg_source_ids, axis=0)
    contract_last = (((1,), (1,)), ((), ()))
    contract_first = (((0,), (0,)), ((), ()))
    target_scores = lax.dot_general(
        query_low, neg_target, contract_last, preferred_element_type=jnp.float32
    )
    source_scores = lax.dot_general(
        probe_low, neg_source, contract_last, preferred_element_type=jnp.float32
    )
    pos_grad = -jax.nn.sigmoid(-positive)
    neg_count = target_scores.shape[1]
    target_weight = (jax.nn.sigmoid(target_scores) / neg_count).astype(jnp.bfloat16)
    source_weight = (jax.nn.sigmoid(source_scores) / neg_count).astype(jnp.bfloat16)
    query_grad = pos_grad[:, None] * target_vec + jnp.dot(
        target_weight, neg_target, preferred_element_type=jnp.float32
    )
    probe_grad = jnp.dot(source_weight, neg_source, preferred_element_type=jnp.float32)
    neg_target_grad = lax.dot_general(
        target_weight, query_low, contract_first, preferred_element_type=jnp.float32
    )
    neg_source_grad = lax.dot_general(
        source_weight, probe_low, contract_first, preferred_element_type=jnp.float32
    )
    source_grad = source_grad.at[pick_source].add(conj_product(query_grad, relation_vec))
    source_grad = source_grad.at[neg_source_ids].add(neg_source_grad)
    target_grad = target_grad.at[pick_target].add(
        pos_grad[:, None] * query + complex_product(probe_grad, relation_vec)
    )
    target_grad = target_grad.at[neg_target_ids].add(neg_target_grad)
    relation_term = conj_product(query_grad, source_vec) + conj_product(target_vec, probe_grad)
    relation_grad = relation_grad.at[pick_relation].add(relation_term)
    return (source_grad, target_grad, relation_grad)


def adagrad(params, state, grad):
    new_state = state + jnp.mean(grad * grad, axis=1)
    new_params = params.astype(jnp.float32) - learn_rate * grad / jnp.sqrt(new_state)[:, None]
    return (new_params, new_state)


def shards(
    source_rows,
    source_state,
    target_rows,
    target_state,
    relations,
    relation_state,
    source_ids,
    relation_ids,
    target_ids,
    source_negs,
    target_negs,
    edge_counts,
):
    part_rows = source_rows.shape[0]
    width = source_rows.shape[1]
    relation_count = relations.shape[0]
    tables = (
        source_rows,
        target_rows,
        relations,
        source_ids,
        relation_ids,
        target_ids,
        source_negs,
        target_negs,
    )
    start = (
        jnp.zeros((part_rows, width), jnp.float32),
        jnp.zeros((part_rows, width), jnp.float32),
        jnp.zeros((relation_count, width), jnp.float32),
    )
    block_count = edge_counts[0] // BLOCK
    source_grad, target_grad, relation_grad = lax.fori_loop(
        jnp.int32(0), block_count, lambda block, carry: block_step(block, carry, tables), start
    )
    new_target, new_target_state = adagrad(target_rows, target_state, target_grad)
    partner_bit = lax.axis_size("blk").bit_length() - 2
    target_out = swapped(new_target.astype(jnp.bfloat16), "blk", partner_bit)
    target_state_out = swapped(new_target_state, "blk", partner_bit)
    summed = lax.psum(relation_grad, ("blk", "grp"))
    relations_out, relation_state_out = adagrad(relations, relation_state, summed)
    new_source, new_source_state = adagrad(source_rows, source_state, source_grad)
    return (
        new_source.astype(jnp.bfloat16),
        new_source_state,
        target_out,
        target_state_out,
        relations_out,
        relation_state_out,
    )


def solution(mesh):
    return jax.shard_map(
        shards,
        mesh=mesh,
        in_specs=(
            P(("blk", "grp"), None),
            P(("blk", "grp")),
            P(("blk", "grp"), None),
            P(("blk", "grp")),
            P(),
            P(),
            P(("blk", "grp")),
            P(("blk", "grp")),
            P(("blk", "grp")),
            P(("blk", "grp"), None),
            P(("blk", "grp"), None),
            P(("blk", "grp")),
        ),
        out_specs=(
            P(("blk", "grp"), None),
            P(("blk", "grp")),
            P(("blk", "grp"), None),
            P(("blk", "grp")),
            P(),
            P(),
        ),
        check_vma=False,
    )
```

profile of v0, /device:TPU:1, one launch (start us, length us, event | category | flops | bytes accessed | tf_op | source)
XLA Modules:
  0.0 1571.5 jit_solution(10509110678641138942)
XLA Ops:
  16.1 1275.4 %while.14 = (s32[]{:T(128)}, f32[1024,400]{1,0:T(8,128)S(1)}, f32[1024,400]{1,0:T(8,128)}, f32[1024,400]{1,0:T(8,128)}, s32[]{:T(128)}, /*index=5*/s32[2048]{0:T...) while((s32[]{:T(128)}, f32[1024,400]{1,0:T(8,128)S(1)}, ...), condition=%wide.region_7.10_spmd, body=%wide.region_0.9_spmd.sunk | while | flops 636018176 | bytes 48617060 | solution.py:143
  71.8 10.1 scatter_fusion.3
  87.8 8.0 scatter_fusion.1
  151.5 10.1 scatter_fusion.3
  231.2 10.1 scatter_fusion.3
  247.2 8.0 scatter_fusion.1
  310.9 10.1 scatter_fusion.3
  326.9 8.0 scatter_fusion.1
  390.6 10.1 scatter_fusion.3
  406.6 8.0 scatter_fusion.1
  470.3 10.1 scatter_fusion.3
  550.1 10.1 scatter_fusion.3
  566.0 8.0 scatter_fusion.1
  629.8 10.1 scatter_fusion.3
  645.7 8.0 scatter_fusion.1
  709.5 10.1 scatter_fusion.3
  789.2 10.1 scatter_fusion.3
  868.9 10.1 scatter_fusion.3
  948.6 10.1 scatter_fusion.3
  1028.3 10.1 scatter_fusion.3
  1108.0 10.1 scatter_fusion.3
  1187.7 10.1 scatter_fusion.3
  1267.4 10.1 scatter_fusion.3
  1313.8 244.3 %all-reduce.2.cloned.1.call-done = f32[1024,400]{0,1:T(8,128)} async-done(((f32[1024,400]{0,1:T(8,128)}), f32[1024,400]{0,1:T(8,128)}) %all-reduce.2.cloned.1.call-update) | async-done | bytes 1638416 | tf_op jit(solution)/shard_map/psum | solution.py:150
  (1706 shorter events, 1096.4 us)
Async XLA Ops:
  7.2 1551.0 %all-reduce.2.cloned.1.call-start = ((), (), s32[]{:S(2)}) async-start(), calls=%async_computation | async-start | bytes 3276800 | tf_op jit(solution)/shard_map/psum | solution.py:150
  71.8 10.1 copy-start.21
  71.8 10.1 copy-start.22
  151.5 10.1 copy-start.21
  151.5 10.1 copy-start.22
  231.2 10.1 copy-start.21
  231.2 10.1 copy-start.22
  310.9 10.1 copy-start.22
  390.6 10.1 copy-start.22
  470.3 10.1 copy-start.22
  550.1 10.1 copy-start.22
  629.8 10.1 copy-start.22
  709.5 10.1 copy-start.22
  789.2 10.1 copy-start.22
  868.9 10.1 copy-start.22
  948.6 10.1 copy-start.22
  1028.3 10.1 copy-start.22
  1108.0 10.1 copy-start.22
  1187.7 10.1 copy-start.22
  1267.4 10.1 copy-start.22
  1300.5 261.5 %collective-permute-start = (bf16[1024,400]{0,1:T(8,128)(2,1)}, bf16[1024,400]{0,1:T(8,128)(2,1)}, u32[]{:S(2)}, u32[]{:S(2)}) collective-permute-start(bf16[1024,400]{0,1:T(8,128)(2,1)} %subtract_convert_fusion.1), channel_id=1, source_target_pairs={{0,128},{128,0},{4,132},{132,4},{8,136},{136,8},{12,140},{140,12},... | collective-permute-start | bytes 2457608 | tf_op jit(solution)/shard_map/ppermute | solution.py:19
  1300.5 13.3 collective-permute-start.1
  1306.6 253.3 %copy-start.41 = (f32[1024]{0:T(1024)S(1)}, f32[1024]{0:T(1024)}, u32[]{:S(2)}) copy-start(f32[1024]{0:T(1024)} %param.23) | copy-start | bytes 12292
  1306.6 253.9 %copy-start.19 = (f32[1024,400]{0,1:T(8,128)S(1)}, f32[1024,400]{0,1:T(8,128)}, u32[]{:S(2)}) copy-start(f32[1024,400]{0,1:T(8,128)} %param.22) | copy-start | bytes 4915204
  (486 other events, 1476.9 us)
Sparse Core Ops, SparseCore 0:
  1294.5 263.5 all-reduce.1
where the time goes:
time: 1590 us; the launch traced here: 1570 us
  other arithmetic  718 us (45%)
  local copies, waits for them, and re-layouts  417 us (26%)
  waiting for transfers between devices  250 us (16%)
  matrix products  162 us (10%)
    psum x1, waiting for transfers between devices, shards(): summed = lax.psum(relation_grad, ('blk', 'grp'))  244 us
    scatter-add x16, other arithmetic, block_step(): target_grad = target_grad.at[neg_target_ids].add(neg_target_grad)  162 us
    scatter-add x16, other arithmetic, block_step(): source_grad = source_grad.at[neg_source_ids].add(neg_source_grad)  128 us
    gather x16, local copies, waits for them, and re-layouts, block_step(): neg_target = jnp.take(target_rows, neg_target_ids, axis=0)  108 us
    gather x16, local copies, waits for them, and re-layouts, block_step(): neg_source = jnp.take(source_rows, neg_source_ids, axis=0)  85.3 us
    gather x32, local copies, waits for them, and re-layouts, block_step(): relation_vec = jnp.take(relations, pick_relation, axis=0)  78.7 us
    scatter-add x16, other arithmetic, block_step(): relation_grad = relation_grad.at[pick_relation].add(relation_term)  74.9 us
    scatter-add x16, other arithmetic, block_step(): target_grad.at[pick_target]  73.3 us
  transfers between devices with their start and end apart: 3, of which 2 were waited for; matrix products, arithmetic and copies ran while one was open for 1% of the time, Pallas kernels for 0%

commit v1 on v0

v1 whole, which is shorter than its diff:
```python
import jax
import jax.numpy as jnp
from jax import lax
from jax.experimental import pallas as pl
from jax.experimental.pallas import tpu as pltpu
from jax.sharding import PartitionSpec as P

F32, BF16 = jnp.float32, jnp.bfloat16
W, HALF, ROWS, EDGES, BLOCK, NEG = 400, 200, 1024, 2048, 128, 1024
CHUNK = 256
PART = 208
RATE = 0.1
NN = (((1,), (0,)), ((), ()))
NT = (((1,), (1,)), ((), ()))
MESH = pl.DeviceIdType.MESH
SIZE = {"y": 4, "x": 4, "z": 8, "core": 2}
HOPS = {"y": (1, 3, 2), "x": (1, 3, 2), "z": (4, 3, 5, 2, 6, 1, 7), "core": (1,)}


def place():
    blk, grp = lax.axis_index("blk"), lax.axis_index("grp")
    return {"y": blk // 16, "x": blk // 4 % 4, "z": grp * 2 + blk // 2 % 2, "core": blk % 2}


def peer(me, axis, hop):
    at = dict(me)
    at[axis] = lax.rem(me[axis] + hop, SIZE[axis])
    return (at["y"] * 16 + at["x"] * 4 + at["z"] % 2 * 2 + at["core"], at["z"] // 2)


def dot(a, b, dims=NN):
    return lax.dot_general(a, b, dims, preferred_element_type=F32)


def mul(a, b):
    ar, ai, br, bi = a[:HALF], a[HALF:], b[:HALF], b[HALF:]
    return jnp.concatenate([ar * br - ai * bi, ar * bi + ai * br], axis=0)


def mulc(a, b):
    ar, ai, br, bi = a[:HALF], a[HALF:], b[:HALF], b[HALF:]
    return jnp.concatenate([ar * br + ai * bi, ai * br - ar * bi], axis=0)


def split(x):
    hi = x.astype(BF16)
    return hi, (x - hi.astype(F32)).astype(BF16)


def one_hot(ids, count):
    at = lax.broadcasted_iota(jnp.int32, (count, ids.shape[1]), 0)
    return jnp.where(at == ids, 1.0, 0.0).astype(BF16)


def counts_of(ids, scale):
    grid = dot(one_hot(ids % 32, 32), one_hot(ids // 32, 32), NT) * scale
    return jnp.concatenate([jnp.broadcast_to(grid[:, h : h + 1], (32, BLOCK)) for h in range(32)], axis=0)


def weights_of(scores, count):
    return (count + count * jnp.tanh(scores)).astype(BF16)


def update(table, state, grad):
    new_state = state + jnp.sum(grad * grad, axis=0, keepdims=True) * (1.0 / W)
    return table - RATE * grad * lax.rsqrt(new_state), new_state


def aligned(index, size):
    return pl.ds(pl.multiple_of(index * size, size), size)


def bucket_kernel(
    live_ref, src_ref, src_state, tgt_ref, tgt_state, rel_ref, sid_ref, rid_ref, did_ref, sneg_ref, tneg_ref,
    src_out, src_state_out, tgt_out, tgt_state_out, rel_sum,
    src_t, tgt_t, rel_hl, oh_s, oh_d, oh_r, w_s, w_t, q_low, p_low, gs_hi, gs_lo, gt_hi, gt_lo, rt,
    tgt_new, tgt_state_new, own, other, from_x, at_z, from_z, at_y, from_y, got_y, got_x, got_core,
    core_s, core_r, x_s, x_r, z_s, z_r, y_s, y_r, gy_s, gy_r, gz_s, gz_r, gx_s, gx_r, gc_s, gc_r,
    t_s, t_r, ts_s, ts_r, out_sem,
):
    me = place()
    core, x, y, z = me["core"], me["x"], me["y"], me["z"]
    barrier = pltpu.get_barrier_semaphore()
    total = 0
    for axis, hops in HOPS.items():
        for hop in hops:
            pl.semaphore_signal(barrier, inc=1, device_id=peer(me, axis, hop), device_id_type=MESH)
            total += 1

    def send(src, dst, send_sem, recv_sem, axis, hop):
        return pltpu.make_async_remote_copy(
            src_ref=src, dst_ref=dst, send_sem=send_sem, recv_sem=recv_sem,
            device_id=peer(me, axis, hop), device_id_type=MESH,
        )

    src_t[...] = (0.5 * src_ref[...].astype(F32)).T.astype(BF16)
    tgt_t[...] = (0.5 * tgt_ref[...].astype(F32)).T.astype(BF16)
    hi, lo = split(rel_ref[...])
    rel_hl[:W] = hi
    rel_hl[W:] = lo
    own[:, W:] = jnp.zeros((8, 2 * PART - W, 128), BF16)
    at_z[:, PART:] = jnp.zeros((2, 256 - PART, 128), BF16)
    count = live_ref[0]

    def edges(c, _):
        first = pl.multiple_of(c * CHUNK, CHUNK)
        here = pl.ds(first, CHUNK)
        scale = jnp.where(first < count, 0.5 / NEG, 0.0).astype(F32)
        alive = jnp.where(first < count, 1.0, 0.0).astype(F32)
        ohs = one_hot(sid_ref[:, here], ROWS)
        ohd = one_hot(did_ref[:, here], ROWS)
        ohr = one_hot(rid_ref[:, here], ROWS)
        oh_s[:, here] = ohs
        oh_d[:, here] = ohd
        oh_r[:, here] = ohr
        s = dot(src_ref[...], ohs)
        d = dot(tgt_ref[...], ohd)
        both = dot(rel_hl[...], ohr)
        r = both[:W] + both[W:]
        q = mul(s, r)
        p = mulc(r, d)
        pos = jnp.sum(q * d, axis=0, keepdims=True)
        pos_grad = -alive / (1.0 + jnp.exp(pos))
        ql = q.astype(BF16)
        plow = p.astype(BF16)
        q_low[:, here] = ql
        p_low[:, here] = plow
        ct = jnp.concatenate([counts_of(tneg_ref[pl.ds(2 * c + i, 1), :], scale) for i in range(2)], axis=1)
        wt = weights_of(dot(tgt_t[...], ql), ct)
        w_t[:, here] = wt
        cs = jnp.concatenate([counts_of(sneg_ref[pl.ds(2 * c + i, 1), :], scale) for i in range(2)], axis=1)
        ws = weights_of(dot(src_t[...], plow), cs)
        w_s[:, here] = ws
        qg = pos_grad * d + dot(tgt_ref[...], wt)
        pg = dot(src_ref[...], ws)
        gs_hi[:, here], gs_lo[:, here] = split(mulc(qg, r))
        gt_hi[:, here], gt_lo[:, here] = split(pos_grad * q + mul(pg, r))
        rt[:, here] = (mulc(qg, s) + mulc(d, pg)).astype(BF16)
        return 0

    lax.fori_loop(0, EDGES // CHUNK, edges, 0)
    pl.semaphore_wait(barrier, total)

    half = aligned(core, PART)
    far = aligned(1 - core, PART)
    order = HOPS["x"] + (0,)

    def piece(i):
        return lax.rem(x + order[i], 4)

    def core_copy(i):
        tiles = pl.ds(2 * piece(i), 2)
        return send(own.at[tiles, far], other.at[tiles], core_s.at[i], core_r.at[i], "core", 1)

    def x_copy(i):
        return send(other.at[pl.ds(2 * piece(i), 2)], from_x.at[i], x_s.at[i], x_r.at[i], "x", order[i])

    def relation_piece(i):
        j = piece(i)
        grad = dot(rt[...], oh_r[aligned(j, CHUNK), :], NT).astype(BF16)
        own[2 * j, :W] = grad[:, :128]
        own[2 * j + 1, :W] = grad[:, 128:]
        core_copy(i).start()

    def core_add(i):
        core_copy(i).wait_recv()
        tiles = pl.ds(2 * piece(i), 2)
        other[tiles] = (other[tiles].astype(F32) + own[tiles, half].astype(F32)).astype(BF16)

    for i in range(4):
        relation_piece(i)
        if i:
            core_add(i - 1)
            x_copy(i - 1).start()
    core_add(3)

    def rows_step(c, table, state, hi_ref, lo_ref, oh, low, wts):
        here = aligned(c, CHUNK)
        grad = dot(hi_ref[...], oh[here, :], NT) + dot(lo_ref[...], oh[here, :], NT) + dot(low[...], wts[here, :], NT)
        return here, update(table[:, here].astype(F32), state[:, here], grad)

    def target_copy(c):
        here = aligned(c, CHUNK)
        return send(tgt_new.at[:, here], tgt_out.at[:, here], t_s.at[c], t_r.at[c], "y", 2)

    def target_step(c, _):
        here, (new, new_state) = rows_step(c, tgt_ref, tgt_state, gt_hi, gt_lo, oh_d, q_low, w_t)
        tgt_new[:, here] = new.astype(BF16)
        tgt_state_new[:, here] = new_state
        target_copy(c).start()
        return 0

    def source_step(c, _):
        here, (new, new_state) = rows_step(c, src_ref, src_state, gs_hi, gs_lo, oh_s, p_low, w_s)
        src_out[:, here] = new.astype(BF16)
        src_state_out[:, here] = new_state
        return 0

    lax.fori_loop(0, 3, target_step, 0)
    for i in range(3):
        x_copy(i).wait_recv()
    mine = pl.ds(2 * x, 2)
    at_z[:, :PART] = (
        other[mine].astype(F32) + from_x[0].astype(F32) + from_x[1].astype(F32) + from_x[2].astype(F32)
    ).astype(BF16)
    z_hops, y_hops = HOPS["z"], HOPS["y"]
    z_copies = []
    for i, hop in enumerate(z_hops):
        to = lax.rem(z + hop, 8)
        z_copies.append(send(at_z.at[to // 4, aligned(to % 4, 64)], from_z.at[i], z_s.at[i], z_r.at[i], "z", hop))
        z_copies[-1].start()
    lax.fori_loop(3, 4, target_step, 0)
    state_copy = send(tgt_state_new, tgt_state_out, ts_s, ts_r, "y", 2)
    state_copy.start()
    for copy in z_copies:
        copy.wait_recv()
    summed = at_z[z // 4, aligned(z % 4, 64), :].astype(F32)
    for i in range(7):
        summed = summed + from_z[i].astype(F32)
    at_y[...] = summed.astype(BF16)
    y_copies = []
    for i, hop in enumerate(y_hops):
        to = lax.rem(y + hop, 4)
        y_copies.append(send(at_y.at[aligned(to, 16)], from_y.at[i], y_s.at[i], y_r.at[i], "y", hop))
        y_copies[-1].start()
    lax.fori_loop(0, 1, source_step, 0)
    for copy in y_copies:
        copy.wait_recv()
    tile = aligned(y, 16)
    summed = at_y[tile, :].astype(F32)
    for i in range(3):
        summed = summed + from_y[i].astype(F32)
    got_y[tile, :] = summed.astype(BF16)
    back_y = []
    for i, hop in enumerate(y_hops):
        back_y.append(send(got_y.at[tile], got_y.at[tile], gy_s.at[i], gy_r.at[i], "y", hop))
        back_y[-1].start()
    lax.fori_loop(1, 2, source_step, 0)
    for copy in back_y:
        copy.wait_recv()
    slot = got_x.at[x, z // 4, aligned(z % 4, 64)]
    back_z = []
    for i, hop in enumerate(z_hops):
        back_z.append(send(got_y, slot, gz_s.at[i], gz_r.at[i], "z", hop))
        back_z[-1].start()
    got_x[x, z // 4, aligned(z % 4, 64), :] = got_y[...]
    lax.fori_loop(2, 3, source_step, 0)
    for copy in back_z:
        copy.wait_recv()
    back_x = []
    for i, hop in enumerate(HOPS["x"]):
        ready = got_x.at[x, :, pl.ds(0, PART)]
        back_x.append(send(ready, ready, gx_s.at[i], gx_r.at[i], "x", hop))
        back_x[-1].start()

    def to_core(i, index):
        return send(got_x.at[index, :, pl.ds(0, PART)], got_core.at[index], gc_s.at[i], gc_r.at[i], "core", 1)

    cores = [to_core(0, x)]
    cores[0].start()
    lax.fori_loop(3, 4, source_step, 0)
    for i, hop in enumerate(HOPS["x"]):
        back_x[i].wait_recv()
        cores.append(to_core(i + 1, lax.rem(x + 4 - hop, 4)))
        cores[-1].start()
    out_own = pltpu.make_async_copy(got_x.at[:, :, pl.ds(0, PART)], rel_sum.at[core], out_sem.at[0])
    out_own.start()
    for copy in cores:
        copy.wait_recv()
    out_far = pltpu.make_async_copy(got_core, rel_sum.at[1 - core], out_sem.at[1])
    out_far.start()
    for i in range(4):
        core_copy(i).wait_send()
        target_copy(i).wait()
    for i in range(3):
        x_copy(i).wait_send()
    for copy in z_copies + y_copies + back_y + back_z + back_x + cores:
        copy.wait_send()
    state_copy.wait()
    out_own.wait()
    out_far.wait()


def finish_kernel(src, src_state, tgt, tgt_state, sums, rel, rel_state,
                  src_out, src_state_out, tgt_out, tgt_state_out, rel_out, rel_state_out, sem):
    copies = [
        pltpu.make_async_copy(a, b, sem.at[i])
        for i, (a, b) in enumerate(
            [(src, src_out), (tgt, tgt_out), (src_state, src_state_out), (tgt_state, tgt_state_out)]
        )
    ]
    for copy in copies:
        copy.start()
    for t in range(8):
        here = slice(128 * t, 128 * t + 128)
        grad = jnp.concatenate([sums[0, t // 2, t % 2], sums[1, t // 2, t % 2, : W - PART]], axis=0).astype(F32)
        new, new_state = update(rel[:, here], rel_state[:, here], grad)
        rel_out[:, here] = new
        rel_state_out[:, here] = new_state
    for copy in copies:
        copy.wait()


def shards(src, src_state, tgt, tgt_state, rel, rel_state, sid, rid, did, sneg, tneg, live):
    vm = pl.BlockSpec(memory_space=pltpu.VMEM)
    sm = pl.BlockSpec(memory_space=pltpu.SMEM)
    hbm = pl.BlockSpec(memory_space=pl.ANY)
    shape = jax.ShapeDtypeStruct
    dma = pltpu.SemaphoreType.DMA

    def vmem(*dims, dtype=BF16):
        return pltpu.VMEM(dims, dtype)

    rows_bf, row_f = shape((W, ROWS), BF16), shape((1, ROWS), F32)
    wide = [(1, ROWS), (1, EDGES)]
    new_src, new_src_state, new_tgt, new_tgt_state, sums = pl.pallas_call(
        bucket_kernel,
        out_shape=(rows_bf, row_f, rows_bf, row_f, shape((2, 4, 2, PART, 128), BF16)),
        in_specs=[sm] + [vm] * 10,
        out_specs=[vm, vm, hbm, hbm, hbm],
        scratch_shapes=[vmem(ROWS, W), vmem(ROWS, W), vmem(2 * W, ROWS)]
        + [vmem(ROWS, EDGES)] * 5
        + [vmem(W, EDGES)] * 7
        + [
            vmem(W, ROWS), vmem(1, ROWS, dtype=F32), vmem(8, 2 * PART, 128), vmem(8, PART, 128),
            vmem(3, 2, PART, 128), vmem(2, 256, 128), vmem(7, 64, 128), vmem(64, 128), vmem(3, 16, 128),
            vmem(64, 128), vmem(4, 2, 256, 128), vmem(4, 2, PART, 128),
        ]
        + [dma((n,)) for n in (4, 4, 3, 3, 7, 7, 3, 3, 3, 3, 7, 7, 3, 3, 4, 4, 4, 4)]
        + [dma(()), dma(()), dma((2,))],
        compiler_params=pltpu.CompilerParams(
            collective_id=0, has_side_effects=True, vmem_limit_bytes=60 * 2**20
        ),
        name="bucket",
    )(live, src.T, src_state.reshape(wide[0]), tgt.T, tgt_state.reshape(wide[0]), rel.T,
      sid.reshape(wide[1]), rid.reshape(wide[1]), did.reshape(wide[1]), sneg, tneg)
    outs = pl.pallas_call(
        finish_kernel,
        out_shape=(rows_bf, row_f, rows_bf, row_f, shape((W, ROWS), F32), row_f),
        in_specs=[vm] * 7,
        out_specs=[hbm] * 4 + [vm] * 2,
        scratch_shapes=[dma((4,))],
        name="finish",
    )(new_src, new_src_state, new_tgt, new_tgt_state, sums, rel.T, rel_state.reshape(wide[0]))
    return (outs[0].T, outs[1].reshape(ROWS), outs[2].T, outs[3].reshape(ROWS), outs[4].T, outs[5].reshape(ROWS))


def solution(mesh):
    split_rows, split_one, copied = P(("blk", "grp"), None), P(("blk", "grp")), P()
    return jax.shard_map(
        shards,
        mesh=mesh,
        in_specs=(split_rows, split_one, split_rows, split_one, copied, copied,
                  split_one, split_one, split_one, split_rows, split_rows, split_one),
        out_specs=(split_rows, split_one, split_rows, split_one, copied, copied),
        check_vma=False,
    )
```

time: 1590 us -> 87.6 us (0.06); the launches traced: 1570 us -> 87.4 us
  other arithmetic: 718 us -> 0 us
  local copies, waits for them, and re-layouts: 417 us -> 0 us
  waiting for transfers between devices: 250 us -> 0 us
  matrix products: 162 us -> 0 us
  Pallas kernels: 0 us -> 86 us
    scatter-add x80 -> x0, other arithmetic: 473 us -> none  [the longest x16 162 us: block_step(): target_grad = target_grad.at[neg_target_ids].add(neg_target_grad)]
    gather x128 -> x0, local copies, waits for them, and re-layouts: 335 us -> none  [the longest x16 108 us: block_step(): neg_target = jnp.take(target_rows, neg_target_ids, axis=0)]
    psum x1 -> x0, waiting for transfers between devices: 244 us -> none  [shards(): summed = lax.psum(relation_grad, ('blk', 'grp'))]
    dot_general x96 -> x0, matrix products: 162 us -> none  [the longest x16 45.2 us: block_step(): lax.dot_general(target_weight, query_low, contract_first, preferred_eleme...]
    pallas_call x0 -> x2, Pallas kernels: none -> 86 us  [the longest x1 81.5 us: shards(): pl.pallas_call(bucket_kernel, out_shape=(rows_bf, row_f, rows_bf, row_f,...]
    and x64 -> x0, other arithmetic: 63.4 us -> none  [the longest x16 20.7 us: block_step(): target_vec = jnp.take(target_rows, pick_target, axis=0).astype(jnp.float32)]
    add x64 -> x0, other arithmetic: 41.1 us -> none  [the longest x32 25.1 us: conj_product(): left_re * right_re + left_im * right_im]
    select_n x32 -> x0, other arithmetic: 37.3 us -> none  [the longest x16 22.1 us: block_step(): target_grad = target_grad.at[neg_target_ids].add(neg_target_grad)]
  transfers between devices with their start and end apart: 3 -> 0, of which waited for: 2 -> 0; matrix products, arithmetic and copies ran while one was open for 1% -> 0% of each run, Pallas kernels for 0% -> 0%
where the time goes in v1:
time: 87.6 us; the launch traced here: 87.4 us
  Pallas kernels  86 us (98%)
  between operations  1.45 us (2%)
    pallas_call x1, Pallas kernels, shards(): pl.pallas_call(bucket_kernel, out_shape=(rows_bf, row_f, rows_bf, row_f,...  81.5 us
    pallas_call x1, Pallas kernels, shards(): pl.pallas_call(finish_kernel, out_shape=(rows_bf, row_f, rows_bf, row_f,...  4.52 us

profile of v1, /device:TPU:1, one launch (start us, length us, event | category | flops | bytes accessed | tf_op | source)
XLA Modules:
  0.0 87.4 jit_solution(15247830587554650513)
XLA Ops:
  1.3 81.5 %bucket.1 = (bf16[400,1024]{1,0:T(8,128)(2,1)}, f32[1,1024]{1,0:T(1,128)}, bf16[400,1024]{1,0:T(8,128)(2,1)}, f32[1,1024]{1,0:T(1,128)}, bf16[2,4,2,208,128]{4,3,2,1,0:T(8,128)(2,1)}) custom-call(s32[1]{0:T(128)S(6)} %copy.18.live_ref, bf16[400,1024]{1,0:T(8,128)(2,1)} %bitcast.17, f32[1,1024]{1,0:T(1,128)} %bitcast.22, bf16[400,1024]{1,0:T(8,128)(2,1)} %bitcast.18, ...), custom_call_target="tpu_custom_call" | custom-call | tf_op jit(solution)/shard_map/bucket/pallas_call | solution.py:316
  82.8 4.5 %finish.1 = (bf16[400,1024]{1,0:T(8,128)(2,1)}, f32[1,1024]{1,0:T(1,128)}, bf16[400,1024]{1,0:T(8,128)(2,1)}, f32[1,1024]{1,0:T(1,128)}, f32[400,1024]{1,0:T(8,128)}, /*index=5*/f32[1,1024]{1,0:T(1,128)}) custom-call(bf16[400,1024]{1,0:T(8,128)(2,1)} %get-tuple-element.17.src, f32[1,1024]{1,0:T(1,128)} %get-tuple-element.18.src_state, ...), custom_call_target="tpu_custom_call" | custom-call | tf_op jit(solution)/shard_map/finish/pallas_call | solution.py:337

commit v2 on v1

--- a/solution.py
+++ b/solution.py
@@ -14,7 +14,7 @@
 NT = (((1,), (1,)), ((), ()))
 MESH = pl.DeviceIdType.MESH
 SIZE = {"y": 4, "x": 4, "z": 8, "core": 2}
-HOPS = {"y": (1, 3, 2), "x": (1, 3, 2), "z": (4, 3, 5, 2, 6, 1, 7), "core": (1,)}
+HOPS = {"y": (2, 1, 3), "x": (2, 1, 3), "z": (4, 3, 5, 2, 6, 1, 7), "core": (1,)}
 
 
 def place():
@@ -52,6 +52,21 @@
     return jnp.where(at == ids, 1.0, 0.0).astype(BF16)
 
 
+def pick(table, ids):
+    low, high = ids % 128, ids // 128
+    parts = []
+    for b in range(ids.shape[1] // 128):
+        lanes = slice(128 * b, 128 * b + 128)
+        at = jnp.broadcast_to(low[:, lanes], (W, 128))
+        tile = jnp.broadcast_to(high[:, lanes], (W, 128))
+        out = jnp.take_along_axis(table[:, :128], at, axis=1, mode="promise_in_bounds")
+        for t in range(1, ROWS // 128):
+            got = jnp.take_along_axis(table[:, 128 * t : 128 * t + 128], at, axis=1, mode="promise_in_bounds")
+            out = jnp.where(tile == t, got, out)
+        parts.append(out)
+    return jnp.concatenate(parts, axis=1)
+
+
 def counts_of(ids, scale):
     grid = dot(one_hot(ids % 32, 32), one_hot(ids // 32, 32), NT) * scale
     return jnp.concatenate([jnp.broadcast_to(grid[:, h : h + 1], (32, BLOCK)) for h in range(32)], axis=0)
@@ -71,13 +86,24 @@
 
 
 def bucket_kernel(
-    live_ref, src_ref, src_state, tgt_ref, tgt_state, rel_ref, sid_ref, rid_ref, did_ref, sneg_ref, tneg_ref,
-    src_out, src_state_out, tgt_out, tgt_state_out, rel_sum,
-    src_t, tgt_t, rel_hl, oh_s, oh_d, oh_r, w_s, w_t, q_low, p_low, gs_hi, gs_lo, gt_hi, gt_lo, rt,
-    tgt_new, tgt_state_new, own, other, from_x, at_z, from_z, at_y, from_y, got_y, got_x, got_core,
-    core_s, core_r, x_s, x_r, z_s, z_r, y_s, y_r, gy_s, gy_r, gz_s, gz_r, gx_s, gx_r, gc_s, gc_r,
-    t_s, t_r, ts_s, ts_r, out_sem,
+    live_ref, src_h, src_state_h, tgt_h, tgt_state_h, rel_h, rel_state_h, sid_h, rid_h, did_h, sneg_h, tneg_h,
+    src_out, src_state_out, tgt_out, tgt_state_out, rel_out, rel_state_out,
+    src_ref, src_state, tgt_ref, tgt_state, rel_ref, rel_state, sid_ref, rid_ref, did_ref, sneg_ref, tneg_ref, in_sem,
+    src_t, tgt_t, oh_s, oh_d, oh_r, w_s, w_t, q_low, p_low, gs_hi, gs_lo, gt_hi, gt_lo, rt,
+    tgt_new, tgt_state_new, own, other, from_x, at_z, from_z, from_y, got_y, got,
+    core_s, core_r, x_s, x_r, z_s, z_r, y_s, y_r, gz_s, gz_r, gx_s, gx_r, gc_s, gc_r,
+    t_s, t_r, ts_s, ts_r,
 ):
+    loads = [
+        pltpu.make_async_copy(here, there, in_sem.at[i])
+        for i, (here, there) in enumerate([
+            (src_h, src_ref), (tgt_h, tgt_ref), (rel_h, rel_ref), (sid_h, sid_ref), (rid_h, rid_ref), (did_h, did_ref),
+            (sneg_h, sneg_ref), (tneg_h, tneg_ref), (src_state_h, src_state), (tgt_state_h, tgt_state),
+            (rel_state_h, rel_state),
+        ])
+    ]
+    for load in loads:
+        load.start()
     me = place()
     core, x, y, z = me["core"], me["x"], me["y"], me["z"]
     barrier = pltpu.get_barrier_semaphore()
@@ -93,13 +119,14 @@
             device_id=peer(me, axis, hop), device_id_type=MESH,
         )
 
-    src_t[...] = (0.5 * src_ref[...].astype(F32)).T.astype(BF16)
-    tgt_t[...] = (0.5 * tgt_ref[...].astype(F32)).T.astype(BF16)
-    hi, lo = split(rel_ref[...])
-    rel_hl[:W] = hi
-    rel_hl[W:] = lo
     own[:, W:] = jnp.zeros((8, 2 * PART - W, 128), BF16)
     at_z[:, PART:] = jnp.zeros((2, 256 - PART, 128), BF16)
+    loads[0].wait()
+    src_t[...] = (0.5 * src_ref[...].astype(F32)).T.astype(BF16)
+    loads[1].wait()
+    tgt_t[...] = (0.5 * tgt_ref[...].astype(F32)).T.astype(BF16)
+    for load in loads[2:]:
+        load.wait()
     count = live_ref[0]
 
     def edges(c, _):
@@ -115,8 +142,7 @@
         oh_r[:, here] = ohr
         s = dot(src_ref[...], ohs)
         d = dot(tgt_ref[...], ohd)
-        both = dot(rel_hl[...], ohr)
-        r = both[:W] + both[W:]
+        r = pick(rel_ref, rid_ref[:, here])
         q = mul(s, r)
         p = mulc(r, d)
         pos = jnp.sum(q * d, axis=0, keepdims=True)
@@ -187,7 +213,6 @@
         here, (new, new_state) = rows_step(c, tgt_ref, tgt_state, gt_hi, gt_lo, oh_d, q_low, w_t)
         tgt_new[:, here] = new.astype(BF16)
         tgt_state_new[:, here] = new_state
-        target_copy(c).start()
         return 0
 
     def source_step(c, _):
@@ -196,7 +221,12 @@
         src_state_out[:, here] = new_state
         return 0
 
-    lax.fori_loop(0, 3, target_step, 0)
+    def target_first(c, _):
+        target_step(c, 0)
+        target_copy(c).start()
+        return 0
+
+    lax.fori_loop(0, 2, target_first, 0)
     for i in range(3):
         x_copy(i).wait_recv()
     mine = pl.ds(2 * x, 2)
@@ -209,139 +239,142 @@
         to = lax.rem(z + hop, 8)
         z_copies.append(send(at_z.at[to // 4, aligned(to % 4, 64)], from_z.at[i], z_s.at[i], z_r.at[i], "z", hop))
         z_copies[-1].start()
-    lax.fori_loop(3, 4, target_step, 0)
-    state_copy = send(tgt_state_new, tgt_state_out, ts_s, ts_r, "y", 2)
-    state_copy.start()
+    lax.fori_loop(2, 4, target_step, 0)
     for copy in z_copies:
         copy.wait_recv()
     summed = at_z[z // 4, aligned(z % 4, 64), :].astype(F32)
     for i in range(7):
         summed = summed + from_z[i].astype(F32)
-    at_y[...] = summed.astype(BF16)
+    from_y[y] = summed.astype(BF16)
     y_copies = []
     for i, hop in enumerate(y_hops):
-        to = lax.rem(y + hop, 4)
-        y_copies.append(send(at_y.at[aligned(to, 16)], from_y.at[i], y_s.at[i], y_r.at[i], "y", hop))
+        y_copies.append(send(from_y.at[y], from_y.at[y], y_s.at[i], y_r.at[i], "y", hop))
         y_copies[-1].start()
     lax.fori_loop(0, 1, source_step, 0)
     for copy in y_copies:
         copy.wait_recv()
-    tile = aligned(y, 16)
-    summed = at_y[tile, :].astype(F32)
-    for i in range(3):
-        summed = summed + from_y[i].astype(F32)
-    got_y[tile, :] = summed.astype(BF16)
-    back_y = []
-    for i, hop in enumerate(y_hops):
-        back_y.append(send(got_y.at[tile], got_y.at[tile], gy_s.at[i], gy_r.at[i], "y", hop))
-        back_y[-1].start()
-    lax.fori_loop(1, 2, source_step, 0)
-    for copy in back_y:
-        copy.wait_recv()
-    slot = got_x.at[x, z // 4, aligned(z % 4, 64)]
+    target_copy(2).start()
+    target_copy(3).start()
+    state_copy = send(tgt_state_new, tgt_state_out, ts_s, ts_r, "y", 2)
+    state_copy.start()
+    summed = from_y[0].astype(F32) + from_y[1].astype(F32) + from_y[2].astype(F32) + from_y[3].astype(F32)
+    got_y[...] = summed.astype(BF16)
+    slot = got.at[core, x, z // 4, aligned(z % 4, 64)]
     back_z = []
     for i, hop in enumerate(z_hops):
         back_z.append(send(got_y, slot, gz_s.at[i], gz_r.at[i], "z", hop))
         back_z[-1].start()
-    got_x[x, z // 4, aligned(z % 4, 64), :] = got_y[...]
-    lax.fori_loop(2, 3, source_step, 0)
+    got[core, x, z // 4, aligned(z % 4, 64), :] = got_y[...]
+    lax.fori_loop(1, 3, source_step, 0)
     for copy in back_z:
         copy.wait_recv()
+
+    def piece_copy(index, send_sem, recv_sem, axis, hop):
+        ready = got.at[core, index, :, pl.ds(0, PART)]
+        return send(ready, ready, send_sem, recv_sem, axis, hop)
+
     back_x = []
     for i, hop in enumerate(HOPS["x"]):
-        ready = got_x.at[x, :, pl.ds(0, PART)]
-        back_x.append(send(ready, ready, gx_s.at[i], gx_r.at[i], "x", hop))
+        back_x.append(piece_copy(x, gx_s.at[i], gx_r.at[i], "x", hop))
         back_x[-1].start()
-
-    def to_core(i, index):
-        return send(got_x.at[index, :, pl.ds(0, PART)], got_core.at[index], gc_s.at[i], gc_r.at[i], "core", 1)
-
-    cores = [to_core(0, x)]
+    arrival = (x,) + tuple(lax.rem(x + 4 - hop, 4) for hop in HOPS["x"])
+    cores = [piece_copy(x, gc_s.at[0], gc_r.at[0], "core", 1)]
     cores[0].start()
     lax.fori_loop(3, 4, source_step, 0)
-    for i, hop in enumerate(HOPS["x"]):
+
+    def relation_rows(i):
+        cores[i].wait_recv()
+        j = arrival[i]
+        for half_tile in range(2):
+            here = aligned(2 * j + half_tile, 128)
+            grad = jnp.concatenate([got[0, j, half_tile, :PART], got[1, j, half_tile, : W - PART]], axis=0).astype(F32)
+            new, new_state = update(rel_ref[:, here], rel_state[:, here], grad)
+            rel_out[:, here] = new
+            rel_state_out[:, here] = new_state
+
+    for i in range(3):
         back_x[i].wait_recv()
-        cores.append(to_core(i + 1, lax.rem(x + 4 - hop, 4)))
+        cores.append(piece_copy(arrival[i + 1], gc_s.at[i + 1], gc_r.at[i + 1], "core", 1))
         cores[-1].start()
-    out_own = pltpu.make_async_copy(got_x.at[:, :, pl.ds(0, PART)], rel_sum.at[core], out_sem.at[0])
-    out_own.start()
-    for copy in cores:
-        copy.wait_recv()
-    out_far = pltpu.make_async_copy(got_core, rel_sum.at[1 - core], out_sem.at[1])
-    out_far.start()
+        relation_rows(i)
+    relation_rows(3)
     for i in range(4):
         core_copy(i).wait_send()
         target_copy(i).wait()
     for i in range(3):
         x_copy(i).wait_send()
-    for copy in z_copies + y_copies + back_y + back_z + back_x + cores:
+    for copy in z_copies + y_copies + back_z + back_x + cores:
         copy.wait_send()
     state_copy.wait()
-    out_own.wait()
-    out_far.wait()
-
-
-def finish_kernel(src, src_state, tgt, tgt_state, sums, rel, rel_state,
-                  src_out, src_state_out, tgt_out, tgt_state_out, rel_out, rel_state_out, sem):
-    copies = [
-        pltpu.make_async_copy(a, b, sem.at[i])
-        for i, (a, b) in enumerate(
-            [(src, src_out), (tgt, tgt_out), (src_state, src_state_out), (tgt_state, tgt_state_out)]
-        )
-    ]
-    for copy in copies:
-        copy.start()
-    for t in range(8):
-        here = slice(128 * t, 128 * t + 128)
-        grad = jnp.concatenate([sums[0, t // 2, t % 2], sums[1, t // 2, t % 2, : W - PART]], axis=0).astype(F32)
-        new, new_state = update(rel[:, here], rel_state[:, here], grad)
-        rel_out[:, here] = new
-        rel_state_out[:, here] = new_state
-    for copy in copies:
-        copy.wait()
+
+
+def finish_kernel(*refs):
+    ins, outs, stages, in_sem, out_sem = refs[:6], refs[6:12], refs[12:18], refs[18], refs[19]
+    loads, stores = [], []
+    for half in range(2):
+        for i, (here, stage, there) in enumerate(zip(ins, stages, outs)):
+            if half and here.shape[0] == 1:
+                continue
+            rows = pl.ds(0, 1) if here.shape[0] == 1 else pl.ds(half * 208, 192 if half else 208)
+            loads.append(pltpu.make_async_copy(here.at[rows], stage.at[rows], in_sem.at[half, i]))
+            stores.append(pltpu.make_async_copy(stage.at[rows], there.at[rows], out_sem.at[half, i]))
+    for load in loads:
+        load.start()
+    for load, store in zip(loads, stores):
+        load.wait()
+        store.start()
+    for store in stores:
+        store.wait()
 
 
 def shards(src, src_state, tgt, tgt_state, rel, rel_state, sid, rid, did, sneg, tneg, live):
     vm = pl.BlockSpec(memory_space=pltpu.VMEM)
     sm = pl.BlockSpec(memory_space=pltpu.SMEM)
-    hbm = pl.BlockSpec(memory_space=pl.ANY)
+    hbm = pl.BlockSpec(memory_space=pltpu.HBM)
     shape = jax.ShapeDtypeStruct
     dma = pltpu.SemaphoreType.DMA
 
     def vmem(*dims, dtype=BF16):
         return pltpu.VMEM(dims, dtype)
 
+    def like(ref):
+        return pltpu.VMEM(ref.shape, ref.dtype)
+
     rows_bf, row_f = shape((W, ROWS), BF16), shape((1, ROWS), F32)
+    rows_f, ids, negs = shape((W, ROWS), F32), shape((1, EDGES), jnp.int32), shape(sneg.shape, jnp.int32)
     wide = [(1, ROWS), (1, EDGES)]
-    new_src, new_src_state, new_tgt, new_tgt_state, sums = pl.pallas_call(
+    results = (rows_bf, row_f, rows_bf, row_f, rows_f, row_f)
+    outs = pl.pallas_call(
         bucket_kernel,
-        out_shape=(rows_bf, row_f, rows_bf, row_f, shape((2, 4, 2, PART, 128), BF16)),
-        in_specs=[sm] + [vm] * 10,
-        out_specs=[vm, vm, hbm, hbm, hbm],
-        scratch_shapes=[vmem(ROWS, W), vmem(ROWS, W), vmem(2 * W, ROWS)]
+        out_shape=results,
+        in_specs=[sm] + [hbm] * 11,
+        out_specs=[vm] * 6,
+        scratch_shapes=[like(r) for r in (*results, ids, ids, ids, negs, negs)]
+        + [dma((11,)), vmem(ROWS, W), vmem(ROWS, W)]
         + [vmem(ROWS, EDGES)] * 5
         + [vmem(W, EDGES)] * 7
         + [
             vmem(W, ROWS), vmem(1, ROWS, dtype=F32), vmem(8, 2 * PART, 128), vmem(8, PART, 128),
-            vmem(3, 2, PART, 128), vmem(2, 256, 128), vmem(7, 64, 128), vmem(64, 128), vmem(3, 16, 128),
-            vmem(64, 128), vmem(4, 2, 256, 128), vmem(4, 2, PART, 128),
+            vmem(3, 2, PART, 128), vmem(2, 256, 128), vmem(7, 64, 128), vmem(4, 64, 128), vmem(64, 128),
+            vmem(2, 4, 2, 256, 128),
         ]
-        + [dma((n,)) for n in (4, 4, 3, 3, 7, 7, 3, 3, 3, 3, 7, 7, 3, 3, 4, 4, 4, 4)]
-        + [dma(()), dma(()), dma((2,))],
+        + [dma((n,)) for n in (4, 4, 3, 3, 7, 7, 3, 3, 7, 7, 3, 3, 4, 4, 4, 4)]
+        + [dma(()), dma(())],
         compiler_params=pltpu.CompilerParams(
             collective_id=0, has_side_effects=True, vmem_limit_bytes=60 * 2**20
         ),
         name="bucket",
-    )(live, src.T, src_state.reshape(wide[0]), tgt.T, tgt_state.reshape(wide[0]), rel.T,
+    )(live, src.T, src_state.reshape(wide[0]), tgt.T, tgt_state.reshape(wide[0]), rel.T, rel_state.reshape(wide[0]),
       sid.reshape(wide[1]), rid.reshape(wide[1]), did.reshape(wide[1]), sneg, tneg)
     outs = pl.pallas_call(
         finish_kernel,
-        out_shape=(rows_bf, row_f, rows_bf, row_f, shape((W, ROWS), F32), row_f),
-        in_specs=[vm] * 7,
-        out_specs=[hbm] * 4 + [vm] * 2,
-        scratch_shapes=[dma((4,))],
+        out_shape=results,
+        in_specs=[hbm] * 6,
+        out_specs=[hbm] * 6,
+        scratch_shapes=[like(r) for r in results] + [dma((2, 6)), dma((2, 6))],
+        compiler_params=pltpu.CompilerParams(vmem_limit_bytes=60 * 2**20),
         name="finish",
-    )(new_src, new_src_state, new_tgt, new_tgt_state, sums, rel.T, rel_state.reshape(wide[0]))
+    )(*outs)
     return (outs[0].T, outs[1].reshape(ROWS), outs[2].T, outs[3].reshape(ROWS), outs[4].T, outs[5].reshape(ROWS))
 
 

time: 87.6 us -> 69.8 us (0.80)
  Pallas kernels: 86 us -> 68.4 us
    pallas_call x2, Pallas kernels: 86 us -> 68.4 us  [the longest x1 65.3 us: shards(): pl.pallas_call(bucket_kernel, out_shape=results, in_specs=[sm] + [hbm] *...]
where the time goes in v2:
time: 69.8 us; the launch traced here: 69.7 us
  Pallas kernels  68.4 us (98%)
  between operations  1.29 us (2%)
    pallas_call x1, Pallas kernels, shards(): pl.pallas_call(bucket_kernel, out_shape=results, in_specs=[sm] + [hbm] *...  65.3 us
    pallas_call x1, Pallas kernels, shards(): pl.pallas_call(finish_kernel, out_shape=results, in_specs=[hbm] * 6, out_...  3.06 us

profile of v2, /device:TPU:1, one launch (start us, length us, event | category | flops | bytes accessed | tf_op | source)
XLA Modules:
  0.0 69.7 jit_solution(2270748159117988559)
XLA Ops:
  1.3 65.3 %bucket.1 = (bf16[400,1024]{1,0:T(8,128)(2,1)}, f32[1,1024]{1,0:T(1,128)}, bf16[400,1024]{1,0:T(8,128)(2,1)}, f32[1,1024]{1,0:T(1,128)}, f32[400,1024]{1,0:T(8,128)}, /*index=5*/f32[1,1024]{1,0:T(1,128)}) custom-call(s32[1]{0:T(128)S(6)} %copy.18.live_ref, bf16[400,1024]{1,0:T(8,128)(2,1)} %bitcast.16, f32[1,1024]{1,0:T(1,128)} %bitcast.21, ...), custom_call_target="tpu_custom_call" | custom-call | tf_op jit(solution)/shard_map/bucket/pallas_call | solution.py:347
  66.6 3.1 %finish.1 = (bf16[400,1024]{1,0:T(8,128)(2,1)}, f32[1,1024]{1,0:T(1,128)}, bf16[400,1024]{1,0:T(8,128)(2,1)}, f32[1,1024]{1,0:T(1,128)}, f32[400,1024]{1,0:T(8,128)}, /*index=5*/f32[1,1024]{1,0:T(1,128)}) custom-call(bf16[400,1024]{1,0:T(8,128)(2,1)} %get-tuple-element.18.refs_0_, f32[1,1024]{1,0:T(1,128)} %get-tuple-element.19.refs_1_, ...), custom_call_target="tpu_custom_call" | custom-call | tf_op jit(solution)/shard_map/finish/pallas_call | solution.py:369

commit v3 on v2

--- a/solution.py
+++ b/solution.py
@@ -8,6 +8,8 @@
 F32, BF16 = jnp.float32, jnp.bfloat16
 W, HALF, ROWS, EDGES, BLOCK, NEG = 400, 200, 1024, 2048, 128, 1024
 CHUNK = 256
+EDGE_CHUNK = 1024
+LANE_ROWS = 320
 PART = 208
 RATE = 0.1
 NN = (((1,), (0,)), ((), ()))
@@ -52,16 +54,16 @@
     return jnp.where(at == ids, 1.0, 0.0).astype(BF16)
 
 
-def pick(table, ids):
+def pick(table, ids, rows):
     low, high = ids % 128, ids // 128
     parts = []
     for b in range(ids.shape[1] // 128):
         lanes = slice(128 * b, 128 * b + 128)
-        at = jnp.broadcast_to(low[:, lanes], (W, 128))
-        tile = jnp.broadcast_to(high[:, lanes], (W, 128))
-        out = jnp.take_along_axis(table[:, :128], at, axis=1, mode="promise_in_bounds")
+        at = jnp.broadcast_to(low[:, lanes], (rows, 128))
+        tile = jnp.broadcast_to(high[:, lanes], (rows, 128))
+        out = jnp.take_along_axis(table[:rows, :128], at, axis=1, mode="promise_in_bounds")
         for t in range(1, ROWS // 128):
-            got = jnp.take_along_axis(table[:, 128 * t : 128 * t + 128], at, axis=1, mode="promise_in_bounds")
+            got = jnp.take_along_axis(table[:rows, 128 * t : 128 * t + 128], at, axis=1, mode="promise_in_bounds")
             out = jnp.where(tile == t, got, out)
         parts.append(out)
     return jnp.concatenate(parts, axis=1)
@@ -89,10 +91,10 @@
     live_ref, src_h, src_state_h, tgt_h, tgt_state_h, rel_h, rel_state_h, sid_h, rid_h, did_h, sneg_h, tneg_h,
     src_out, src_state_out, tgt_out, tgt_state_out, rel_out, rel_state_out,
     src_ref, src_state, tgt_ref, tgt_state, rel_ref, rel_state, sid_ref, rid_ref, did_ref, sneg_ref, tneg_ref, in_sem,
-    src_t, tgt_t, oh_s, oh_d, oh_r, w_s, w_t, q_low, p_low, gs_hi, gs_lo, gt_hi, gt_lo, rt,
-    tgt_new, tgt_state_new, own, other, from_x, at_z, from_z, from_y, got_y, got,
+    src_t, tgt_t, rel_hl, oh_s, oh_d, oh_r, w_s, w_t, q_low, p_low, gs_hi, gs_lo, gt_hi, gt_lo, rt,
+    own, other, from_x, at_z, from_z, from_y, got_y, got,
     core_s, core_r, x_s, x_r, z_s, z_r, y_s, y_r, gz_s, gz_r, gx_s, gx_r, gc_s, gc_r,
-    t_s, t_r, ts_s, ts_r,
+    t_s, t_r, so_sem, ro_sem, ts_s, ts_r, state_sem,
 ):
     loads = [
         pltpu.make_async_copy(here, there, in_sem.at[i])
@@ -127,13 +129,22 @@
     tgt_t[...] = (0.5 * tgt_ref[...].astype(F32)).T.astype(BF16)
     for load in loads[2:]:
         load.wait()
+    rel_hl[: W - LANE_ROWS], rel_hl[W - LANE_ROWS :] = split(rel_ref[LANE_ROWS:])
     count = live_ref[0]
 
     def edges(c, _):
-        first = pl.multiple_of(c * CHUNK, CHUNK)
-        here = pl.ds(first, CHUNK)
-        scale = jnp.where(first < count, 0.5 / NEG, 0.0).astype(F32)
-        alive = jnp.where(first < count, 1.0, 0.0).astype(F32)
+        first = pl.multiple_of(c * EDGE_CHUNK, EDGE_CHUNK)
+        here = pl.ds(first, EDGE_CHUNK)
+        slots = first + lax.broadcasted_iota(jnp.int32, (1, EDGE_CHUNK), 1)
+        alive = jnp.where(slots < count, 1.0, 0.0).astype(F32)
+
+        def block_counts(negs):
+            blocks = []
+            for i in range(EDGE_CHUNK // BLOCK):
+                scale = jnp.where(first + i * BLOCK < count, 0.5 / NEG, 0.0).astype(F32)
+                blocks.append(counts_of(negs[pl.ds(c * (EDGE_CHUNK // BLOCK) + i, 1), :], scale))
+            return jnp.concatenate(blocks, axis=1)
+
         ohs = one_hot(sid_ref[:, here], ROWS)
         ohd = one_hot(did_ref[:, here], ROWS)
         ohr = one_hot(rid_ref[:, here], ROWS)
@@ -142,7 +153,10 @@
         oh_r[:, here] = ohr
         s = dot(src_ref[...], ohs)
         d = dot(tgt_ref[...], ohd)
-        r = pick(rel_ref, rid_ref[:, here])
+        low = dot(rel_hl[...], ohr)
+        r = jnp.concatenate(
+            [pick(rel_ref, rid_ref[:, here], LANE_ROWS), low[: W - LANE_ROWS] + low[W - LANE_ROWS :]], axis=0
+        )
         q = mul(s, r)
         p = mulc(r, d)
         pos = jnp.sum(q * d, axis=0, keepdims=True)
@@ -151,11 +165,9 @@
         plow = p.astype(BF16)
         q_low[:, here] = ql
         p_low[:, here] = plow
-        ct = jnp.concatenate([counts_of(tneg_ref[pl.ds(2 * c + i, 1), :], scale) for i in range(2)], axis=1)
-        wt = weights_of(dot(tgt_t[...], ql), ct)
+        wt = weights_of(dot(tgt_t[...], ql), block_counts(tneg_ref))
         w_t[:, here] = wt
-        cs = jnp.concatenate([counts_of(sneg_ref[pl.ds(2 * c + i, 1), :], scale) for i in range(2)], axis=1)
-        ws = weights_of(dot(src_t[...], plow), cs)
+        ws = weights_of(dot(src_t[...], plow), block_counts(sneg_ref))
         w_s[:, here] = ws
         qg = pos_grad * d + dot(tgt_ref[...], wt)
         pg = dot(src_ref[...], ws)
@@ -164,7 +176,7 @@
         rt[:, here] = (mulc(qg, s) + mulc(d, pg)).astype(BF16)
         return 0
 
-    lax.fori_loop(0, EDGES // CHUNK, edges, 0)
+    lax.fori_loop(0, EDGES // EDGE_CHUNK, edges, 0)
     pl.semaphore_wait(barrier, total)
 
     half = aligned(core, PART)
@@ -207,18 +219,23 @@
 
     def target_copy(c):
         here = aligned(c, CHUNK)
-        return send(tgt_new.at[:, here], tgt_out.at[:, here], t_s.at[c], t_r.at[c], "y", 2)
+        return send(tgt_ref.at[:, here], tgt_out.at[:, here], t_s.at[c], t_r.at[c], "y", 2)
 
     def target_step(c, _):
         here, (new, new_state) = rows_step(c, tgt_ref, tgt_state, gt_hi, gt_lo, oh_d, q_low, w_t)
-        tgt_new[:, here] = new.astype(BF16)
-        tgt_state_new[:, here] = new_state
+        tgt_ref[:, here] = new.astype(BF16)
+        tgt_state[:, here] = new_state
         return 0
+
+    def source_copy(c):
+        here = aligned(c, CHUNK)
+        return pltpu.make_async_copy(src_ref.at[:, here], src_out.at[:, here], so_sem.at[c])
 
     def source_step(c, _):
         here, (new, new_state) = rows_step(c, src_ref, src_state, gs_hi, gs_lo, oh_s, p_low, w_s)
-        src_out[:, here] = new.astype(BF16)
-        src_state_out[:, here] = new_state
+        src_ref[:, here] = new.astype(BF16)
+        src_state[:, here] = new_state
+        source_copy(c).start()
         return 0
 
     def target_first(c, _):
@@ -255,7 +272,7 @@
         copy.wait_recv()
     target_copy(2).start()
     target_copy(3).start()
-    state_copy = send(tgt_state_new, tgt_state_out, ts_s, ts_r, "y", 2)
+    state_copy = send(tgt_state, tgt_state_out, ts_s, ts_r, "y", 2)
     state_copy.start()
     summed = from_y[0].astype(F32) + from_y[1].astype(F32) + from_y[2].astype(F32) + from_y[3].astype(F32)
     got_y[...] = summed.astype(BF16)
@@ -282,6 +299,13 @@
     cores[0].start()
     lax.fori_loop(3, 4, source_step, 0)
 
+    source_state_copy = pltpu.make_async_copy(src_state, src_state_out, state_sem.at[0])
+    source_state_copy.start()
+
+    def relation_copy(i):
+        here = aligned(arrival[i], CHUNK)
+        return pltpu.make_async_copy(rel_ref.at[:, here], rel_out.at[:, here], ro_sem.at[i])
+
     def relation_rows(i):
         cores[i].wait_recv()
         j = arrival[i]
@@ -289,8 +313,9 @@
             here = aligned(2 * j + half_tile, 128)
             grad = jnp.concatenate([got[0, j, half_tile, :PART], got[1, j, half_tile, : W - PART]], axis=0).astype(F32)
             new, new_state = update(rel_ref[:, here], rel_state[:, here], grad)
-            rel_out[:, here] = new
-            rel_state_out[:, here] = new_state
+            rel_ref[:, here] = new
+            rel_state[:, here] = new_state
+        relation_copy(i).start()
 
     for i in range(3):
         back_x[i].wait_recv()
@@ -298,7 +323,11 @@
         cores[-1].start()
         relation_rows(i)
     relation_rows(3)
+    relation_state_copy = pltpu.make_async_copy(rel_state, rel_state_out, state_sem.at[1])
+    relation_state_copy.start()
+    source_state_copy.wait()
     for i in range(4):
+        source_copy(i).wait()
         core_copy(i).wait_send()
         target_copy(i).wait()
     for i in range(3):
@@ -306,18 +335,24 @@
     for copy in z_copies + y_copies + back_z + back_x + cores:
         copy.wait_send()
     state_copy.wait()
+    for i in range(4):
+        relation_copy(i).wait()
+    relation_state_copy.wait()
 
 
 def finish_kernel(*refs):
     ins, outs, stages, in_sem, out_sem = refs[:6], refs[6:12], refs[12:18], refs[18], refs[19]
     loads, stores = [], []
-    for half in range(2):
+    for part in range(2):
         for i, (here, stage, there) in enumerate(zip(ins, stages, outs)):
-            if half and here.shape[0] == 1:
-                continue
-            rows = pl.ds(0, 1) if here.shape[0] == 1 else pl.ds(half * 208, 192 if half else 208)
-            loads.append(pltpu.make_async_copy(here.at[rows], stage.at[rows], in_sem.at[half, i]))
-            stores.append(pltpu.make_async_copy(stage.at[rows], there.at[rows], out_sem.at[half, i]))
+            if here.shape[0] == 1:
+                if part:
+                    continue
+                rows = pl.ds(0, 1)
+            else:
+                rows = pl.ds(part * 208, 192 if part else 208)
+            loads.append(pltpu.make_async_copy(here.at[rows], stage.at[rows], in_sem.at[part, i]))
+            stores.append(pltpu.make_async_copy(stage.at[rows], there.at[rows], out_sem.at[part, i]))
     for load in loads:
         load.start()
     for load, store in zip(loads, stores):
@@ -328,7 +363,6 @@
 
 
 def shards(src, src_state, tgt, tgt_state, rel, rel_state, sid, rid, did, sneg, tneg, live):
-    vm = pl.BlockSpec(memory_space=pltpu.VMEM)
     sm = pl.BlockSpec(memory_space=pltpu.SMEM)
     hbm = pl.BlockSpec(memory_space=pltpu.HBM)
     shape = jax.ShapeDtypeStruct
@@ -348,18 +382,18 @@
         bucket_kernel,
         out_shape=results,
         in_specs=[sm] + [hbm] * 11,
-        out_specs=[vm] * 6,
+        out_specs=[hbm] * 6,
         scratch_shapes=[like(r) for r in (*results, ids, ids, ids, negs, negs)]
-        + [dma((11,)), vmem(ROWS, W), vmem(ROWS, W)]
+        + [dma((11,)), vmem(ROWS, W), vmem(ROWS, W), vmem(2 * (W - LANE_ROWS), ROWS)]
         + [vmem(ROWS, EDGES)] * 5
         + [vmem(W, EDGES)] * 7
         + [
-            vmem(W, ROWS), vmem(1, ROWS, dtype=F32), vmem(8, 2 * PART, 128), vmem(8, PART, 128),
+            vmem(8, 2 * PART, 128), vmem(8, PART, 128),
             vmem(3, 2, PART, 128), vmem(2, 256, 128), vmem(7, 64, 128), vmem(4, 64, 128), vmem(64, 128),
             vmem(2, 4, 2, 256, 128),
         ]
-        + [dma((n,)) for n in (4, 4, 3, 3, 7, 7, 3, 3, 7, 7, 3, 3, 4, 4, 4, 4)]
-        + [dma(()), dma(())],
+        + [dma((n,)) for n in (4, 4, 3, 3, 7, 7, 3, 3, 7, 7, 3, 3, 4, 4, 4, 4, 4, 4)]
+        + [dma(()), dma(()), dma((2,))],
         compiler_params=pltpu.CompilerParams(
             collective_id=0, has_side_effects=True, vmem_limit_bytes=60 * 2**20
         ),

time: 69.8 us -> 66.8 us (0.957)
  Pallas kernels: 68.4 us -> 65.3 us
    pallas_call x1, Pallas kernels: 65.3 us -> 62.2 us  [shards(): pl.pallas_call(bucket_kernel, out_shape=results, in_specs=[sm] + [hbm] *...]
where the time goes in v3:
time: 66.8 us; the launch traced here: 66.7 us
  Pallas kernels  65.3 us (98%)
  between operations  1.45 us (2%)
    pallas_call x1, Pallas kernels, shards(): pl.pallas_call(bucket_kernel, out_shape=results, in_specs=[sm] + [hbm] *...  62.2 us
    pallas_call x1, Pallas kernels, shards(): pl.pallas_call(finish_kernel, out_shape=results, in_specs=[hbm] * 6, out_...  3.06 us

profile of v3, /device:TPU:1, one launch (start us, length us, event | category | flops | bytes accessed | tf_op | source)
XLA Modules:
  0.0 66.7 jit_solution(14289658114916661008)
XLA Ops:
  1.3 62.2 %bucket.1 = (bf16[400,1024]{1,0:T(8,128)(2,1)}, f32[1,1024]{1,0:T(1,128)}, bf16[400,1024]{1,0:T(8,128)(2,1)}, f32[1,1024]{1,0:T(1,128)}, f32[400,1024]{1,0:T(8,128)}, /*index=5*/f32[1,1024]{1,0:T(1,128)}) custom-call(s32[1]{0:T(128)S(6)} %copy.18.live_ref, bf16[400,1024]{1,0:T(8,128)(2,1)} %bitcast.16, f32[1,1024]{1,0:T(1,128)} %bitcast.21, ...), custom_call_target="tpu_custom_call" | custom-call | tf_op jit(solution)/shard_map/bucket/pallas_call | solution.py:381
  63.5 3.1 %finish.1 = (bf16[400,1024]{1,0:T(8,128)(2,1)}, f32[1,1024]{1,0:T(1,128)}, bf16[400,1024]{1,0:T(8,128)(2,1)}, f32[1,1024]{1,0:T(1,128)}, f32[400,1024]{1,0:T(8,128)}, /*index=5*/f32[1,1024]{1,0:T(1,128)}) custom-call(bf16[400,1024]{1,0:T(8,128)(2,1)} %get-tuple-element.18.refs_0_, f32[1,1024]{1,0:T(1,128)} %get-tuple-element.19.refs_1_, ...), custom_call_target="tpu_custom_call" | custom-call | tf_op jit(solution)/shard_map/finish/pallas_call | solution.py:403

commit v4 on v3

--- a/solution.py
+++ b/solution.py
@@ -270,59 +270,76 @@
     lax.fori_loop(0, 1, source_step, 0)
     for copy in y_copies:
         copy.wait_recv()
+    summed = from_y[0].astype(F32) + from_y[1].astype(F32) + from_y[2].astype(F32) + from_y[3].astype(F32)
+    got_y[...] = summed.astype(BF16)
+    slot = got.at[core, x, z // 4, aligned(z % 4, 64)]
+
+    def z_back(hop):
+        return send(got_y, slot, gz_s.at[hop], gz_r.at[hop], "z", hop)
+
+    for hop in z_hops:
+        z_back(hop).start()
+    got[core, x, z // 4, aligned(z % 4, 64), :] = got_y[...]
     target_copy(2).start()
     target_copy(3).start()
     state_copy = send(tgt_state, tgt_state_out, ts_s, ts_r, "y", 2)
     state_copy.start()
-    summed = from_y[0].astype(F32) + from_y[1].astype(F32) + from_y[2].astype(F32) + from_y[3].astype(F32)
-    got_y[...] = summed.astype(BF16)
-    slot = got.at[core, x, z // 4, aligned(z % 4, 64)]
-    back_z = []
-    for i, hop in enumerate(z_hops):
-        back_z.append(send(got_y, slot, gz_s.at[i], gz_r.at[i], "z", hop))
-        back_z[-1].start()
-    got[core, x, z // 4, aligned(z % 4, 64), :] = got_y[...]
     lax.fori_loop(1, 3, source_step, 0)
-    for copy in back_z:
-        copy.wait_recv()
-
-    def piece_copy(index, send_sem, recv_sem, axis, hop):
-        ready = got.at[core, index, :, pl.ds(0, PART)]
+
+    lane_tile = (z // 4, 1 - z // 4)
+
+    def tile_copy(k, index, send_sem, recv_sem, axis, hop):
+        ready = got.at[core, index, lane_tile[k], pl.ds(0, PART)]
         return send(ready, ready, send_sem, recv_sem, axis, hop)
 
-    back_x = []
-    for i, hop in enumerate(HOPS["x"]):
-        back_x.append(piece_copy(x, gx_s.at[i], gx_r.at[i], "x", hop))
-        back_x[-1].start()
     arrival = (x,) + tuple(lax.rem(x + 4 - hop, 4) for hop in HOPS["x"])
-    cores = [piece_copy(x, gc_s.at[0], gc_r.at[0], "core", 1)]
-    cores[0].start()
+
+    def x_back(k, i):
+        return tile_copy(k, x, gx_s.at[3 * k + i], gx_r.at[3 * k + i], "x", HOPS["x"][i])
+
+    def core_back(k, i):
+        return tile_copy(k, arrival[i], gc_s.at[4 * k + i], gc_r.at[4 * k + i], "core", 1)
+
+    for k in range(2):
+        for step in range(1 - k, 4):
+            owner = lane_tile[k] * 4 + (z + step) % 4
+            hop = lax.rem(z - owner + 8, 8)
+            pltpu.make_async_remote_copy(
+                src_ref=got_y, dst_ref=got.at[core, x, owner // 4, aligned(owner % 4, 64)],
+                send_sem=gz_s.at[hop], recv_sem=gz_r.at[hop],
+                device_id=peer(me, "z", hop), device_id_type=MESH,
+            ).wait_recv()
+        for i in range(3):
+            x_back(k, i).start()
+        core_back(k, 0).start()
     lax.fori_loop(3, 4, source_step, 0)
 
     source_state_copy = pltpu.make_async_copy(src_state, src_state_out, state_sem.at[0])
     source_state_copy.start()
 
-    def relation_copy(i):
-        here = aligned(arrival[i], CHUNK)
-        return pltpu.make_async_copy(rel_ref.at[:, here], rel_out.at[:, here], ro_sem.at[i])
-
-    def relation_rows(i):
-        cores[i].wait_recv()
-        j = arrival[i]
-        for half_tile in range(2):
-            here = aligned(2 * j + half_tile, 128)
-            grad = jnp.concatenate([got[0, j, half_tile, :PART], got[1, j, half_tile, : W - PART]], axis=0).astype(F32)
-            new, new_state = update(rel_ref[:, here], rel_state[:, here], grad)
-            rel_ref[:, here] = new
-            rel_state[:, here] = new_state
-        relation_copy(i).start()
-
-    for i in range(3):
-        back_x[i].wait_recv()
-        cores.append(piece_copy(arrival[i + 1], gc_s.at[i + 1], gc_r.at[i + 1], "core", 1))
-        cores[-1].start()
-        relation_rows(i)
-    relation_rows(3)
+    def relation_copy(k, i):
+        here = aligned(2 * arrival[i] + lane_tile[k], 128)
+        return pltpu.make_async_copy(rel_ref.at[:, here], rel_out.at[:, here], ro_sem.at[4 * k + i])
+
+    def relation_rows(k, i):
+        core_back(k, i).wait_recv()
+        j, t = arrival[i], lane_tile[k]
+        here = aligned(2 * j + t, 128)
+        grad = jnp.concatenate([got[0, j, t, :PART], got[1, j, t, : W - PART]], axis=0).astype(F32)
+        new, new_state = update(rel_ref[:, here], rel_state[:, here], grad)
+        rel_ref[:, here] = new
+        rel_state[:, here] = new_state
+        relation_copy(k, i).start()
+
+    relation_rows(0, 0)
+    waiting = (1, 0)
+    for k in range(2):
+        for i in range(3):
+            x_back(k, i).wait_recv()
+            core_back(k, i + 1).start()
+            relation_rows(*waiting)
+            waiting = (k, i + 1)
+    relation_rows(*waiting)
     relation_state_copy = pltpu.make_async_copy(rel_state, rel_state_out, state_sem.at[1])
     relation_state_copy.start()
     source_state_copy.wait()
@@ -332,11 +349,19 @@
         target_copy(i).wait()
     for i in range(3):
         x_copy(i).wait_send()
-    for copy in z_copies + y_copies + back_z + back_x + cores:
+    for copy in z_copies + y_copies:
         copy.wait_send()
+    for hop in z_hops:
+        z_back(hop).wait_send()
+    for k in range(2):
+        for i in range(3):
+            x_back(k, i).wait_send()
+        for i in range(4):
+            core_back(k, i).wait_send()
     state_copy.wait()
-    for i in range(4):
-        relation_copy(i).wait()
+    for k in range(2):
+        for i in range(4):
+            relation_copy(k, i).wait()
     relation_state_copy.wait()
 
 
@@ -392,7 +417,7 @@
             vmem(3, 2, PART, 128), vmem(2, 256, 128), vmem(7, 64, 128), vmem(4, 64, 128), vmem(64, 128),
             vmem(2, 4, 2, 256, 128),
         ]
-        + [dma((n,)) for n in (4, 4, 3, 3, 7, 7, 3, 3, 7, 7, 3, 3, 4, 4, 4, 4, 4, 4)]
+        + [dma((n,)) for n in (4, 4, 3, 3, 7, 7, 3, 3, 8, 8, 6, 6, 8, 8, 4, 4, 4, 8)]
         + [dma(()), dma(()), dma((2,))],
         compiler_params=pltpu.CompilerParams(
             collective_id=0, has_side_effects=True, vmem_limit_bytes=60 * 2**20

time: 66.8 us -> 66.5 us (level)
  no operation moved by 1% of the time
where the time goes in v4:
time: 66.5 us; the launch traced here: 66.3 us
  Pallas kernels  64.9 us (98%)
  between operations  1.45 us (2%)
    pallas_call x1, Pallas kernels, shards(): pl.pallas_call(bucket_kernel, out_shape=results, in_specs=[sm] + [hbm] *...  61.8 us
    pallas_call x1, Pallas kernels, shards(): pl.pallas_call(finish_kernel, out_shape=results, in_specs=[hbm] * 6, out_...  3.06 us

profile of v4, /device:TPU:1, one launch (start us, length us, event | category | flops | bytes accessed | tf_op | source)
XLA Modules:
  0.0 66.3 jit_solution(566927808430736830)
XLA Ops:
  1.3 61.8 %bucket.1 = (bf16[400,1024]{1,0:T(8,128)(2,1)}, f32[1,1024]{1,0:T(1,128)}, bf16[400,1024]{1,0:T(8,128)(2,1)}, f32[1,1024]{1,0:T(1,128)}, f32[400,1024]{1,0:T(8,128)}, /*index=5*/f32[1,1024]{1,0:T(1,128)}) custom-call(s32[1]{0:T(128)S(6)} %copy.18.live_ref, bf16[400,1024]{1,0:T(8,128)(2,1)} %bitcast.16, f32[1,1024]{1,0:T(1,128)} %bitcast.21, ...), custom_call_target="tpu_custom_call" | custom-call | tf_op jit(solution)/shard_map/bucket/pallas_call | solution.py:406
  63.1 3.1 %finish.1 = (bf16[400,1024]{1,0:T(8,128)(2,1)}, f32[1,1024]{1,0:T(1,128)}, bf16[400,1024]{1,0:T(8,128)(2,1)}, f32[1,1024]{1,0:T(1,128)}, f32[400,1024]{1,0:T(8,128)}, /*index=5*/f32[1,1024]{1,0:T(1,128)}) custom-call(bf16[400,1024]{1,0:T(8,128)(2,1)} %get-tuple-element.18.refs_0_, f32[1,1024]{1,0:T(1,128)} %get-tuple-element.19.refs_1_, ...), custom_call_target="tpu_custom_call" | custom-call | tf_op jit(solution)/shard_map/finish/pallas_call | solution.py:428

commit v5 on v4

--- a/solution.py
+++ b/solution.py
@@ -190,8 +190,13 @@
         tiles = pl.ds(2 * piece(i), 2)
         return send(own.at[tiles, far], other.at[tiles], core_s.at[i], core_r.at[i], "core", 1)
 
-    def x_copy(i):
-        return send(other.at[pl.ds(2 * piece(i), 2)], from_x.at[i], x_s.at[i], x_r.at[i], "x", order[i])
+    tile_out = (1 - z // 4, z // 4)
+
+    def x_copy(i, k):
+        return send(
+            other.at[2 * piece(i) + tile_out[k]], from_x.at[i, tile_out[k]],
+            x_s.at[2 * i + k], x_r.at[2 * i + k], "x", order[i],
+        )
 
     def relation_piece(i):
         j = piece(i)
@@ -209,7 +214,8 @@
         relation_piece(i)
         if i:
             core_add(i - 1)
-            x_copy(i - 1).start()
+            x_copy(i - 1, 0).start()
+            x_copy(i - 1, 1).start()
     core_add(3)
 
     def rows_step(c, table, state, hi_ref, lo_ref, oh, low, wts):
@@ -244,24 +250,27 @@
         return 0
 
     lax.fori_loop(0, 2, target_first, 0)
-    for i in range(3):
-        x_copy(i).wait_recv()
-    mine = pl.ds(2 * x, 2)
-    at_z[:, :PART] = (
-        other[mine].astype(F32) + from_x[0].astype(F32) + from_x[1].astype(F32) + from_x[2].astype(F32)
-    ).astype(BF16)
     z_hops, y_hops = HOPS["z"], HOPS["y"]
-    z_copies = []
-    for i, hop in enumerate(z_hops):
-        to = lax.rem(z + hop, 8)
-        z_copies.append(send(at_z.at[to // 4, aligned(to % 4, 64)], from_z.at[i], z_s.at[i], z_r.at[i], "z", hop))
-        z_copies[-1].start()
+
+    def z_copy(tile, owner, hop):
+        return send(at_z.at[tile, aligned(owner % 4, 64)], from_z.at[hop], z_s.at[hop], z_r.at[hop], "z", hop)
+
+    for k in range(2):
+        for i in range(3):
+            x_copy(i, k).wait_recv()
+        t = tile_out[k]
+        at_z[t, :PART] = (
+            other[2 * x + t].astype(F32) + from_x[0, t].astype(F32) + from_x[1, t].astype(F32) + from_x[2, t].astype(F32)
+        ).astype(BF16)
+        for step in range(k, 4):
+            owner = t * 4 + (z + step) % 4
+            z_copy(t, owner, lax.rem(owner - z + 8, 8)).start()
     lax.fori_loop(2, 4, target_step, 0)
-    for copy in z_copies:
-        copy.wait_recv()
+    for hop in range(1, 8):
+        z_copy(0, 0, hop).wait_recv()
     summed = at_z[z // 4, aligned(z % 4, 64), :].astype(F32)
-    for i in range(7):
-        summed = summed + from_z[i].astype(F32)
+    for hop in range(1, 8):
+        summed = summed + from_z[hop].astype(F32)
     from_y[y] = summed.astype(BF16)
     y_copies = []
     for i, hop in enumerate(y_hops):
@@ -348,9 +357,12 @@
         core_copy(i).wait_send()
         target_copy(i).wait()
     for i in range(3):
-        x_copy(i).wait_send()
-    for copy in z_copies + y_copies:
+        for k in range(2):
+            x_copy(i, k).wait_send()
+    for copy in y_copies:
         copy.wait_send()
+    for hop in range(1, 8):
+        z_copy(0, 0, hop).wait_send()
     for hop in z_hops:
         z_back(hop).wait_send()
     for k in range(2):
@@ -414,10 +426,10 @@
         + [vmem(W, EDGES)] * 7
         + [
             vmem(8, 2 * PART, 128), vmem(8, PART, 128),
-            vmem(3, 2, PART, 128), vmem(2, 256, 128), vmem(7, 64, 128), vmem(4, 64, 128), vmem(64, 128),
+            vmem(3, 2, PART, 128), vmem(2, 256, 128), vmem(8, 64, 128), vmem(4, 64, 128), vmem(64, 128),
             vmem(2, 4, 2, 256, 128),
         ]
-        + [dma((n,)) for n in (4, 4, 3, 3, 7, 7, 3, 3, 8, 8, 6, 6, 8, 8, 4, 4, 4, 8)]
+        + [dma((n,)) for n in (4, 4, 6, 6, 8, 8, 3, 3, 8, 8, 6, 6, 8, 8, 4, 4, 4, 8)]
         + [dma(()), dma(()), dma((2,))],
         compiler_params=pltpu.CompilerParams(
             collective_id=0, has_side_effects=True, vmem_limit_bytes=60 * 2**20

time: 66.5 us -> 65.9 us (level)
  no operation moved by 1% of the time
where the time goes in v5:
time: 65.9 us; the launch traced here: 65.8 us
  Pallas kernels  64.3 us (98%)
  between operations  1.45 us (2%)
    pallas_call x1, Pallas kernels, shards(): pl.pallas_call(bucket_kernel, out_shape=results, in_specs=[sm] + [hbm] *...  61.3 us
    pallas_call x1, Pallas kernels, shards(): pl.pallas_call(finish_kernel, out_shape=results, in_specs=[hbm] * 6, out_...  3.06 us

profile of v5, /device:TPU:1, one launch (start us, length us, event | category | flops | bytes accessed | tf_op | source)
XLA Modules:
  0.0 65.8 jit_solution(14888389129178587499)
XLA Ops:
  1.3 61.3 %bucket.1 = (bf16[400,1024]{1,0:T(8,128)(2,1)}, f32[1,1024]{1,0:T(1,128)}, bf16[400,1024]{1,0:T(8,128)(2,1)}, f32[1,1024]{1,0:T(1,128)}, f32[400,1024]{1,0:T(8,128)}, /*index=5*/f32[1,1024]{1,0:T(1,128)}) custom-call(s32[1]{0:T(128)S(6)} %copy.18.live_ref, bf16[400,1024]{1,0:T(8,128)(2,1)} %bitcast.16, f32[1,1024]{1,0:T(1,128)} %bitcast.21, ...), custom_call_target="tpu_custom_call" | custom-call | tf_op jit(solution)/shard_map/bucket/pallas_call | solution.py:418
  62.5 3.1 %finish.1 = (bf16[400,1024]{1,0:T(8,128)(2,1)}, f32[1,1024]{1,0:T(1,128)}, bf16[400,1024]{1,0:T(8,128)(2,1)}, f32[1,1024]{1,0:T(1,128)}, f32[400,1024]{1,0:T(8,128)}, /*index=5*/f32[1,1024]{1,0:T(1,128)}) custom-call(bf16[400,1024]{1,0:T(8,128)(2,1)} %get-tuple-element.18.refs_0_, f32[1,1024]{1,0:T(1,128)} %get-tuple-element.19.refs_1_, ...), custom_call_target="tpu_custom_call" | custom-call | tf_op jit(solution)/shard_map/finish/pallas_call | solution.py:440
